TPU v7x, 32 devices: a whole 2x2x4 slice. The times are simulated.
32 devices in a mesh: mom: 4 (over y, x), trow: 4 (over z), tcol: 2 (over core).
Axes of the slice: x: 2, y: 2, z: 4, core: 2. Of those that a mesh axis runs over, the one named last changes fastest.
Arguments:
- g_free: float32 [2, 4, 1536, 1536], P(None, 'mom', 'tcol', 'trow'), may hold values from -6 to 6
- g_greater_t: float32 [2, 4, 1536, 1536], P(None, 'mom', 'tcol', 'trow'), may hold values from -6 to 6
- momentum_map: int32 [4], replicated, may hold values from 0 to 3, each once
- weights: float32 [1536], replicated, may hold values from 0.00076546555 to 0.0076546553
Outputs:
- g_out: float32 [2, 4, 1536, 1536], P(None, 'mom', 'tcol', 'trow')
Inputs may be any that keep to these rules, and one draw needn't show every extreme that they name: `momentum_map`: each number appears once.
All inputs are finite; a program needn't handle non-finite values.
Results may differ from a plain program's by a relative error of at most 0.00022.
Values sent between devices are 32-bit elements; how exact they have to be, the bound alone decides.
A program may use at most 128 MiB of HBM per device.

v0:
```python
import math

import jax
import jax.numpy as jnp
from jax import lax
from jax.sharding import PartitionSpec as P

LY = 4
ITERS = 2


highest = lax.Precision.HIGHEST


def matmul(left_side, right_side):
    return jnp.dot(left_side, right_side, precision=highest, preferred_element_type=jnp.float32)


def phase_tables(momentum_map):
    momenta = momentum_map.shape[0]
    across = momenta // LY
    site_index = jnp.arange(momenta, dtype=jnp.int32)
    wave_x = momentum_map % across
    wave_y = momentum_map // across
    site_x = site_index % across
    site_y = site_index // across
    phase_turns = (
        site_x[:, None] * wave_x[None, :] % across * LY
        + site_y[:, None] * wave_y[None, :] % LY * across
    )
    angles = phase_turns.astype(jnp.float32) * (2.0 * math.pi / momenta)
    norm_scale = 1.0 / math.sqrt(momenta)
    return (jnp.cos(angles) * norm_scale, jnp.sin(angles) * norm_scale)


def mirrored(cosine_table, sine_table, real_part, imag_part):
    return (
        matmul(cosine_table, real_part) + matmul(sine_table, imag_part),
        matmul(cosine_table, imag_part) - matmul(sine_table, real_part),
    )


def self_energy(cosine_table, sine_table, lesser_real, lesser_imag, mirror_real, mirror_imag):
    space_real = matmul(cosine_table, lesser_real) - matmul(sine_table, lesser_imag)
    space_imag = matmul(sine_table, lesser_real) + matmul(cosine_table, lesser_imag)
    square_real = space_real * space_real - space_imag * space_imag
    square_imag = 2.0 * space_real * space_imag
    source_real = square_real * mirror_real - square_imag * mirror_imag
    source_imag = square_real * mirror_imag + square_imag * mirror_real
    sigma_real = matmul(cosine_table.T, source_real) + matmul(sine_table.T, source_imag)
    sigma_imag = matmul(cosine_table.T, source_imag) - matmul(sine_table.T, source_real)
    return jnp.stack([sigma_real, sigma_imag])


def contract(left_side, right_side):
    return jnp.einsum(
        "krs,ksc->krc", left_side, right_side, precision=highest, preferred_element_type=jnp.float32
    )


def weighted_product(sigma_part, green_part):
    real_part = contract(sigma_part[0], green_part[0]) - contract(sigma_part[1], green_part[1])
    imag_part = contract(sigma_part[0], green_part[1]) + contract(sigma_part[1], green_part[0])
    return jnp.stack([real_part, imag_part])


def time_product(sigma_tile, green_tile, weights):
    sigma_rows = lax.all_gather(sigma_tile, "trow", axis=3, tiled=True) * weights
    return weighted_product(sigma_rows, lax.all_gather(green_tile, "tcol", axis=2, tiled=True))


def body(g_free, g_greater_t, momentum_map, weights):
    cosine_table, sine_table = phase_tables(momentum_map)
    momenta = cosine_table.shape[0]
    groups = lax.axis_size("mom")
    local_mom = g_free.shape[1]
    tile_rows = g_free.shape[2]
    tile_cols = g_free.shape[3]
    slab_width = tile_rows * tile_cols // groups

    def to_slabs(tile):
        return tile.reshape(2, local_mom, groups, slab_width)

    greater_slab = lax.all_to_all(
        to_slabs(g_greater_t), "mom", split_axis=2, concat_axis=1, tiled=True
    )
    kept_real, kept_imag = mirrored(
        cosine_table, sine_table, greater_slab[0, :, 0], greater_slab[1, :, 0]
    )
    green_now = g_free
    for sweep in range(ITERS):
        lesser = lax.all_to_all(to_slabs(green_now), "mom", split_axis=2, concat_axis=1, tiled=True)
        piece_width = lesser.shape[3]
        sigma_sigma_slab = self_energy(
            cosine_table, sine_table, lesser[0, :, 0], lesser[1, :, 0], kept_real, kept_imag
        )
        returned = lax.all_to_all(
            sigma_sigma_slab.reshape(2, momenta, 1, piece_width),
            "mom",
            split_axis=1,
            concat_axis=2,
            tiled=True,
        )
        sigma_tile = returned.reshape(2, local_mom, tile_rows, tile_cols)
        green_now = g_free + time_product(sigma_tile, green_now, weights)
    return green_now


def solution(mesh):
    placed = (P(None, "mom", "tcol", "trow"), P(None, "mom", "tcol", "trow"), P(), P())
    return jax.shard_map(
        body, mesh=mesh, in_specs=placed, out_specs=P(None, "mom", "tcol", "trow"), check_vma=False
    )
```

profile of v0, /device:TPU:0, one launch (start us, length us, event | category | flops | bytes accessed | tf_op | source)
XLA Modules:
  0.0 694.3 jit_solution(1640873435013903056)
XLA Ops:
  12.2 5.2 all-to-all-start
  20.8 4.9 copy.9
  25.7 19.4 %all-to-all-done = f32[2,1,4,73728]{3,0,1,2:T(2,128)S(1)} async-done(((f32[2,1,4,73728]{3,0,1,2:T(2,128)}), f32[2,1,4,73728]{3,0,1,2:T(2,128)S(1)}, u32[]{:S(2)}, u32[]{:S(2)}) %all-to-all-start) | async-done | bytes 2359328 | tf_op jit(solution)/shard_map/all_to_all | solution.py:92
  45.0 4.5 all-to-all-start.1
  59.0 17.7 %all-to-all-done.1 = f32[2,1,4,73728]{3,0,1,2:T(2,128)} async-done(((f32[2,1,4,73728]{3,0,1,2:T(2,128)}), f32[2,1,4,73728]{3,0,1,2:T(2,128)}, u32[]{:S(2)}, u32[]{:S(2)}) %all-to-all-start.1) | async-done | bytes 2359328 | tf_op jit(solution)/shard_map/all_to_all | solution.py:84
  76.7 4.5 fusion.159
  95.2 5.2 multiply_subtract_fusion.2
  113.3 30.1 %all_to_all.20 = f32[2,4,1,73728]{3,0,2,1:T(2,128)S(1)} all-to-all(f32[2,4,1,73728]{3,0,2,1:T(2,128)S(1)} %copy.10), channel_id=1, replica_groups=mesh['mom'=4,'trow'=4,'tcol'=2] {'mom'}, dimensions={1} | all-to-all | bytes 4718592 | tf_op jit(solution)/shard_map/all_to_all | solution.py:97
  148.4 166.0 %all-gather.5.cloned.1.call-done = f32[2,1,768,1536]{3,2,0,1:T(8,128)} async-done(((f32[2,1,768,384]{3,2,0,1:T(8,128)}), f32[2,1,768,1536]{3,2,0,1:T(8,128)}) %all-gather.5.cloned.1.call-update) | async-done | bytes 9437200 | tf_op jit(solution)/shard_map/all_gather | solution.py:68
  314.5 9.5 %broadcast_multiply_fusion.1 = f32[2,1,768,1536]{3,2,0,1:T(8,128)} fusion(f32[2,1,768,1536]{3,2,0,1:T(8,128)} %all-gather.5.cloned.1.call-done, f32[1536]{0:T(1024)S(1)} %copy-done.9), kind=kLoop, calls=%fused_computation.19 | loop fusion | flops 2359296 | bytes 18880512 | tf_op jit(solution)/shard_map/mul | solution.py:68
  323.9 4.7 all-gather.7.cloned.1.call-done
  328.7 9.9 %fusion.4 = f32[768,384]{1,0:T(8,128)S(1)} fusion(f32[2,1,768,1536]{3,2,0,1:T(8,128)} %broadcast_multiply_fusion.1, f32[2,1,1536,384]{3,2,1,0:T(8,128)} %all-gather.7.cloned.1.call-done), kind=kOutput, calls=%fused_computation.20 | convolution fusion | flops 5435817984 | bytes 8257536 | tf_op jit(solution)/shard_map/krs,ksc->krc/dot_general | solution.py:56
  338.6 10.9 %fusion.5 = f32[768,384]{1,0:T(8,128)S(1)} fusion(f32[2,1,768,1536]{3,2,0,1:T(8,128)} %broadcast_multiply_fusion.1, f32[2,1,1536,384]{3,2,1,0:T(8,128)} %all-gather.7.cloned.1.call-done), kind=kOutput, calls=%fused_computation.21 | convolution fusion | flops 5435817984 | bytes 8257536 | tf_op jit(solution)/shard_map/krs,ksc->krc/dot_general | solution.py:56
  349.5 7.5 %fusion.19 = f32[1,1,768,384]{3,2,1,0:T(8,128)S(1)} fusion(f32[768,384]{1,0:T(8,128)S(1)} %fusion.4, f32[2,1,1536,384]{3,2,1,0:T(8,128)S(1)} %copy-done.3, f32[2,1,768,1536]{3,2,0,1:T(8,128)S(1)} %copy-done.1), kind=kOutput, calls=%fused_computation.43 | convolution fusion | flops 5436112896 | bytes 9437184 | tf_op jit(solution)/shard_map/krs,ksc->krc/dot_general | solution.py:56
  357.0 7.7 %fusion.17 = f32[1,1,768,384]{3,2,1,0:T(8,128)S(1)} fusion(f32[768,384]{1,0:T(8,128)S(1)} %fusion.5, f32[2,1,1536,384]{3,2,1,0:T(8,128)S(1)} %copy-done.3, f32[2,1,768,1536]{3,2,0,1:T(8,128)S(1)} %copy-done.1), kind=kOutput, calls=%fused_computation.41 | convolution fusion | flops 5436112896 | bytes 9437184 | tf_op jit(solution)/shard_map/krs,ksc->krc/dot_general | solution.py:56
  373.4 32.4 %all_to_all.21 = f32[2,1,4,73728]{3,0,1,2:T(2,128)S(1)} all-to-all(f32[2,1,4,73728]{3,0,1,2:T(2,128)S(1)} %copy.12), channel_id=1, replica_groups=mesh['mom'=4,'trow'=4,'tcol'=2] {'mom'}, dimensions={2} | all-to-all | bytes 4718592 | tf_op jit(solution)/shard_map/all_to_all | solution.py:92
  432.8 29.9 %all_to_all.22 = f32[2,4,1,73728]{3,0,2,1:T(2,128)S(1)} all-to-all(f32[2,4,1,73728]{3,0,2,1:T(2,128)S(1)} %copy.13), channel_id=1, replica_groups=mesh['mom'=4,'trow'=4,'tcol'=2] {'mom'}, dimensions={1} | all-to-all | bytes 4718592 | tf_op jit(solution)/shard_map/all_to_all | solution.py:97
  470.2 165.8 %all-gather.9.cloned.1.call-done = f32[2,1,768,1536]{3,2,0,1:T(8,128)} async-done(((f32[2,1,768,384]{3,2,0,1:T(8,128)}), f32[2,1,768,1536]{3,2,0,1:T(8,128)}) %all-gather.9.cloned.1.call-update) | async-done | bytes 9437200 | tf_op jit(solution)/shard_map/all_gather | solution.py:68
  636.0 9.4 %broadcast_multiply_fusion = f32[2,1,768,1536]{3,2,0,1:T(8,128)} fusion(f32[2,1,768,1536]{3,2,0,1:T(8,128)} %all-gather.9.cloned.1.call-done, f32[1536]{0:T(1024)S(1)} %copy-done.9), kind=kLoop, calls=%fused_computation.18 | loop fusion | flops 2359296 | bytes 18880512 | tf_op jit(solution)/shard_map/mul | solution.py:68
  645.5 4.6 all-gather.11.cloned.1.call-done
  650.1 9.9 %fusion.8 = f32[768,384]{1,0:T(8,128)S(1)} fusion(f32[2,1,768,1536]{3,2,0,1:T(8,128)} %broadcast_multiply_fusion, f32[2,1,1536,384]{3,2,1,0:T(8,128)} %all-gather.11.cloned.1.call-done), kind=kOutput, calls=%fused_computation.24 | convolution fusion | flops 5435817984 | bytes 8257536 | tf_op jit(solution)/shard_map/krs,ksc->krc/dot_general | solution.py:56
  660.0 10.7 %fusion.9 = f32[768,384]{1,0:T(8,128)S(1)} fusion(f32[2,1,768,1536]{3,2,0,1:T(8,128)} %broadcast_multiply_fusion, f32[2,1,1536,384]{3,2,1,0:T(8,128)} %all-gather.11.cloned.1.call-done), kind=kOutput, calls=%fused_computation.25 | convolution fusion | flops 5435817984 | bytes 8257536 | tf_op jit(solution)/shard_map/krs,ksc->krc/dot_general | solution.py:56
  670.7 7.5 %fusion.15 = f32[1,1,768,384]{3,2,1,0:T(8,128)S(1)} fusion(f32[768,384]{1,0:T(8,128)S(1)} %fusion.8, f32[2,1,1536,384]{3,2,1,0:T(8,128)S(1)} %copy-done.4, f32[2,1,768,1536]{3,2,0,1:T(8,128)S(1)} %copy-done), kind=kOutput, calls=%fused_computation.39 | convolution fusion | flops 5436112896 | bytes 9437184 | tf_op jit(solution)/shard_map/krs,ksc->krc/dot_general | solution.py:56
  678.3 7.5 %fusion.13 = f32[1,1,768,384]{3,2,1,0:T(8,128)S(1)} fusion(f32[768,384]{1,0:T(8,128)S(1)} %fusion.9, f32[2,1,1536,384]{3,2,1,0:T(8,128)S(1)} %copy-done.4, f32[2,1,768,1536]{3,2,0,1:T(8,128)S(1)} %copy-done), kind=kOutput, calls=%fused_computation.37 | convolution fusion | flops 5436112896 | bytes 9437184 | tf_op jit(solution)/shard_map/krs,ksc->krc/dot_general | solution.py:56
  (64 shorter events, 95.0 us)
Async XLA Ops:
  12.2 32.8 %all-to-all-start = ((f32[2,1,4,73728]{3,0,1,2:T(2,128)}), f32[2,1,4,73728]{3,0,1,2:T(2,128)S(1)}, u32[]{:S(2)}, u32[]{:S(2)}) async-start(f32[2,1,4,73728]{3,0,1,2:T(2,128)} %copy.8), calls=%async_computation | async-start | bytes 4718592 | tf_op jit(solution)/shard_map/all_to_all | solution.py:92
  45.0 31.7 %all-to-all-start.1 = ((f32[2,1,4,73728]{3,0,1,2:T(2,128)}), f32[2,1,4,73728]{3,0,1,2:T(2,128)}, u32[]{:S(2)}, u32[]{:S(2)}) async-start(f32[2,1,4,73728]{3,0,1,2:T(2,128)} %copy.9), calls=%async_computation.1 | async-start | bytes 4718592 | tf_op jit(solution)/shard_map/all_to_all | solution.py:84
  49.5 2.1 copy-start.8
  49.6 264.9 %all-gather.5.cloned.1.call-start = ((), (), s32[]{:S(2)}) async-start(), calls=%async_computation.5 | async-start | bytes 11796480 | tf_op jit(solution)/shard_map/all_gather | solution.py:68
  86.8 2.8 copy-start.6
  89.6 2.8 copy-start.5
  147.6 166.8 %copy-start.9 = (f32[1536]{0:T(1024)S(1)}, f32[1536]{0:T(1024)}, u32[]{:S(2)}) copy-start(f32[1536]{0:T(1024)} %param.7) | copy-start | bytes 18436
  147.6 181.0 %all-gather.7.cloned.1.call-start = ((), (), s32[]{:S(2)}) async-start(), calls=%async_computation.6 | async-start | bytes 7077888 | tf_op jit(solution)/shard_map/all_gather | solution.py:69
  148.4 487.6 %all-gather.9.cloned.1.call-start = ((), (), s32[]{:S(2)}) async-start(), calls=%async_computation.7 | async-start | bytes 11796480 | tf_op jit(solution)/shard_map/all_gather | solution.py:68
  328.7 20.8 %copy-start.1 = (f32[2,1,768,1536]{3,2,0,1:T(8,128)S(1)}, f32[2,1,768,1536]{3,2,0,1:T(8,128)}, u32[]{:S(2)}) copy-start(f32[2,1,768,1536]{3,2,0,1:T(8,128)} %broadcast_multiply_fusion.1) | copy-start | bytes 28311556
  338.5 10.9 %copy-start.3 = (f32[2,1,1536,384]{3,2,1,0:T(8,128)S(1)}, f32[2,1,1536,384]{3,2,1,0:T(8,128)}, u32[]{:S(2)}) copy-start(f32[2,1,1536,384]{3,2,1,0:T(8,128)} %all-gather.7.cloned.1.call-done) | copy-start | bytes 14155780
  357.0 7.7 %copy-start.2 = (f32[2,1,768,384]{3,2,1,0:T(8,128)S(1)}, f32[2,1,768,384]{3,2,1,0:T(8,128)}, u32[]{:S(2)}) copy-start(f32[2,1,768,384]{3,2,1,0:T(8,128)} %param.4) | copy-start | bytes 7077892
  412.9 2.9 copy-start.7
  469.6 180.5 %all-gather.11.cloned.1.call-start = ((), (), s32[]{:S(2)}) async-start(), calls=%async_computation.8 | async-start | bytes 7077888 | tf_op jit(solution)/shard_map/all_gather | solution.py:69
  650.1 20.6 %copy-start = (f32[2,1,768,1536]{3,2,0,1:T(8,128)S(1)}, f32[2,1,768,1536]{3,2,0,1:T(8,128)}, u32[]{:S(2)}) copy-start(f32[2,1,768,1536]{3,2,0,1:T(8,128)} %broadcast_multiply_fusion) | copy-start | bytes 28311556
  660.0 10.8 %copy-start.4 = (f32[2,1,1536,384]{3,2,1,0:T(8,128)S(1)}, f32[2,1,1536,384]{3,2,1,0:T(8,128)}, u32[]{:S(2)}) copy-start(f32[2,1,1536,384]{3,2,1,0:T(8,128)} %all-gather.11.cloned.1.call-done) | copy-start | bytes 14155780
Sparse Core Ops, SparseCore 0:
  147.7 166.6 all-gather.4
  316.0 12.6 all-gather.6
  469.8 166.2 all-gather.8
  637.4 12.6 all-gather.10
where the time goes:
time: 699 us; the launch traced here: 694 us
  waiting for transfers between devices  380 us (54%)
  matrix products  131 us (19%)
  blocking collectives  92.4 us (13%)
  local copies, waits for them, and re-layouts  43.7 us (6%)
  other arithmetic  23.5 us (3%)
  between operations  13.8 us (2%)
  starting transfers between devices  10 us (1%)
    all_gather x2, waiting for transfers between devices, time_product(): lax.all_gather(sigma_tile, 'trow', axis=3, tiled=True) * weights  332 us
    dot_general x8, matrix products, contract(): jnp.einsum('krs,ksc->krc', left_side, right_side, precision=highest, pref...  71.6 us
    all_to_all x2, blocking collectives, body(): lax.all_to_all(sigma_sigma_slab.reshape(2, momenta, 1, piece_width), 'mom...  60 us
    dot_general x20, matrix products, matmul(): jnp.dot(left_side, right_side, precision=highest, preferred_element_type=...  59.8 us
    all_to_all x1, blocking collectives, body(): lax.all_to_all(to_slabs(green_now), 'mom', split_axis=2, concat_axis=1, t...  32.4 us
    reshape x6, local copies, waits for them, and re-layouts, to_slabs(): return tile.reshape(2, local_mom, groups, slab_width)  20.8 us
    all_to_all x1, waiting for transfers between devices, body(): lax.all_to_all(to_slabs(green_now), 'mom', split_axis=2, concat_axis=1, t...  19.4 us
    mul x2, other arithmetic, time_product(): lax.all_gather(sigma_tile, 'trow', axis=3, tiled=True) * weights  18.9 us
  transfers between devices with their start and end apart: 6, of which 6 were waited for; matrix products, arithmetic and copies ran while one was open for 5% of the time, Pallas kernels for 0%

commit v1 on v0

v1 whole, which is shorter than its diff:
```python
import functools
import math

import jax
import jax.numpy as jnp
from jax import lax
from jax.experimental import pallas as pl
from jax.experimental.pallas import tpu as pltpu
from jax.sharding import PartitionSpec as P

LY = 4
ITERS = 2
CHUNKS = 4
SUBLANES = 8


def phase_tables(momentum_map):
    momenta = momentum_map.shape[0]
    across = momenta // LY
    site_index = jnp.arange(momenta, dtype=jnp.int32)
    wave_x = momentum_map % across
    wave_y = momentum_map // across
    site_x = site_index % across
    site_y = site_index // across
    phase_turns = (
        site_x[:, None] * wave_x[None, :] % across * LY
        + site_y[:, None] * wave_y[None, :] % LY * across
    )
    angles = phase_turns.astype(jnp.float32) * (2.0 * math.pi / momenta)
    norm_scale = 1.0 / math.sqrt(momenta)
    return (jnp.cos(angles) * norm_scale, jnp.sin(angles) * norm_scale)


def over_sites(momenta, one_site):
    if momenta <= 8:
        for site in range(momenta):
            one_site(site, site == 0)
    else:
        one_site(0, True)
        pl.loop(1, momenta)(lambda site: one_site(site, False))


def transform(cos_ref, sin_ref, site, reals, imags, sign):
    total_real = total_imag = None
    for k, (real, imag) in enumerate(zip(reals, imags)):
        c = cos_ref[site, k]
        s = sin_ref[site, k]
        if sign < 0:
            term_real, term_imag = c * real + s * imag, c * imag - s * real
        else:
            term_real, term_imag = c * real - s * imag, c * imag + s * real
        total_real = term_real if k == 0 else total_real + term_real
        total_imag = term_imag if k == 0 else total_imag + term_imag
    return total_real, total_imag


def momentum_values(refs, local_mom, rows):
    reals = [ref[0, j, rows, :] for ref in refs for j in range(local_mom)]
    imags = [ref[1, j, rows, :] for ref in refs for j in range(local_mom)]
    return reals, imags


def mirror_kernel(groups, local_mom, *refs):
    cos_ref, sin_ref = refs[:2]
    ins = refs[2 : 2 + groups]
    out = refs[2 + groups]
    height = out.shape[2]

    @pl.loop(0, height // SUBLANES)
    def _(step):
        rows = pl.ds(pl.multiple_of(step * SUBLANES, SUBLANES), SUBLANES)
        reals, imags = momentum_values(ins, local_mom, rows)

        def one_site(site, first):
            real, imag = transform(cos_ref, sin_ref, site, reals, imags, -1)
            out[0, site, rows, :] = real
            out[1, site, rows, :] = imag

        over_sites(groups * local_mom, one_site)


def sigma_kernel(groups, local_mom, *refs):
    cos_ref, sin_ref = refs[:2]
    ins = refs[2 : 2 + groups]
    mirror = refs[2 + groups]
    outs = refs[3 + groups :]
    height = mirror.shape[2]
    momenta = groups * local_mom

    @pl.loop(0, height // SUBLANES)
    def _(step):
        rows = pl.ds(pl.multiple_of(step * SUBLANES, SUBLANES), SUBLANES)
        reals, imags = momentum_values(ins, local_mom, rows)
        held = {}

        def one_site(site, first):
            a, b = transform(cos_ref, sin_ref, site, reals, imags, 1)
            square_real = a * a - b * b
            square_imag = 2.0 * a * b
            m_real = mirror[0, site, rows, :]
            m_imag = mirror[1, site, rows, :]
            source_real = square_real * m_real - square_imag * m_imag
            source_imag = square_real * m_imag + square_imag * m_real
            for k in range(momenta):
                c = cos_ref[site, k]
                s = sin_ref[site, k]
                term = (c * source_real + s * source_imag, c * source_imag - s * source_real)
                if momenta <= 8:
                    held[k] = term if first else (held[k][0] + term[0], held[k][1] + term[1])
                else:
                    ref, j = outs[k // local_mom], k % local_mom
                    for part in range(2):
                        before = 0.0 if first else ref[part, j, rows, :]
                        ref[part, j, rows, :] = before + term[part]

        over_sites(momenta, one_site)
        for k, term in held.items():
            ref, j = outs[k // local_mom], k % local_mom
            ref[0, j, rows, :] = term[0]
            ref[1, j, rows, :] = term[1]


def call_local(kernel, tables, operands, shapes):
    smem = pl.BlockSpec(memory_space=pltpu.SMEM)
    vmem = pl.BlockSpec(memory_space=pltpu.VMEM)
    cells = math.prod(operands[0].shape) * len(operands)
    return pl.pallas_call(
        kernel,
        out_shape=[jax.ShapeDtypeStruct(s, jnp.float32) for s in shapes],
        in_specs=[smem, smem] + [vmem] * len(operands),
        out_specs=[vmem] * len(shapes),
        compiler_params=pltpu.CompilerParams(vmem_limit_bytes=32 * 2**20),
        cost_estimate=pl.CostEstimate(flops=40 * cells, bytes_accessed=12 * cells, transcendentals=0),
    )(*tables, *operands)


def body(g_free, g_greater_t, momentum_map, weights):
    cosine_table, sine_table = phase_tables(momentum_map)
    groups = lax.axis_size("mom")
    me = lax.axis_index("mom")
    line = lax.axis_size("trow")
    place = lax.axis_index("trow")
    _, local_mom, tile_rows, tile_cols = g_free.shape
    momenta = groups * local_mom
    half = line // 2
    chunks = CHUNKS
    while tile_rows % (chunks * groups * SUBLANES):
        chunks -= 1
    piece_rows = tile_rows // (chunks * groups)
    chunk_rows = piece_rows * groups
    part_cols = half * tile_cols

    def rolled(rows_first, start):
        shape = rows_first.shape
        cut = rows_first.reshape((chunks, groups, piece_rows) + shape[1:])
        twice = jnp.concatenate([cut, cut], axis=1)
        return lax.dynamic_slice_in_dim(twice, start, groups, 1).reshape(shape)

    def rotate(tile, axis):
        return jnp.moveaxis(rolled(jnp.moveaxis(tile, axis, 0), me), 0, axis)

    def unrotate(tile, axis):
        back = lax.rem(groups - me, groups)
        return jnp.moveaxis(rolled(jnp.moveaxis(tile, axis, 0), back), 0, axis)

    order = (me - jnp.arange(groups, dtype=jnp.int32)) % groups
    columns = (order[:, None] * local_mom + jnp.arange(local_mom, dtype=jnp.int32)).reshape(-1)
    tables = (jnp.take(cosine_table, columns, axis=1), jnp.take(sine_table, columns, axis=1))

    def shifted(value, by):
        if by % groups == 0:
            return value
        return lax.ppermute(value, "mom", [(i, (i + by) % groups) for i in range(groups)])

    def to_sites(chunk):
        return [
            shifted(chunk[:, :, s * piece_rows : (s + 1) * piece_rows], s) for s in range(groups)
        ]

    def to_momentum(pieces):
        return jnp.concatenate([shifted(p, -s) for s, p in enumerate(pieces)], axis=2)

    inward = [(j, j + 1) for j in range(half - 1)] + [(j, j - 1) for j in range(half + 1, line)]
    across = [(half - 1, half), (half, half - 1)]
    low = place < half
    distance = jnp.where(low, half - 1 - place, place - half)

    def near_tiles(tile):
        tiles = [tile]
        for _ in range(half - 1):
            tiles.append(lax.ppermute(tiles[-1], "trow", inward))
        return tiles

    def all_times(sigma):
        near = near_tiles(sigma)
        far = [lax.ppermute(t, "trow", across) for t in near]
        blocks = [jnp.where(low, a, b) for a, b in zip(near[::-1] + far, far[::-1] + near)]
        joined = jnp.concatenate(blocks, axis=3) * weights
        return jnp.concatenate([joined[0], joined[1]], axis=1)

    def outward(tiles):
        result = tiles[0]
        for d in range(1, half):
            moving = tiles[d]
            for step in range(1, d + 1):
                pairs = [(half - step, half - 1 - step), (half - 1 + step, half + step)]
                moving = lax.ppermute(moving, "trow", pairs)
            result = jnp.where(distance == d, moving, result)
        return result

    free = rotate(g_free, 2)
    greater = rotate(g_greater_t, 2)

    def chunk_of(tile, axis, c):
        return lax.slice_in_dim(tile, c * chunk_rows, (c + 1) * chunk_rows, axis=axis)

    piece = (2, local_mom, piece_rows, tile_cols)
    greens = [chunk_of(free, 2, c) for c in range(chunks)]
    near_free = near_tiles(g_free)
    hub_plain = jnp.concatenate([t[0] for t in near_free] + [t[1] for t in near_free], axis=2)
    hub_free = rotate(hub_plain, 1)
    right_side = lax.all_gather(hub_plain, "tcol", axis=1, tiled=True)
    mirrors = []
    for sweep in range(ITERS):
        hub_chunks, next_greens = [], []
        for c in range(chunks):
            lesser = to_sites(greens[c])
            if sweep == 0:
                mirrors.append(
                    call_local(
                        functools.partial(mirror_kernel, groups, local_mom),
                        tables,
                        to_sites(chunk_of(greater, 2, c)),
                        [(2, momenta, piece_rows, tile_cols)],
                    )[0]
                )
            sigma = to_momentum(
                call_local(
                    functools.partial(sigma_kernel, groups, local_mom),
                    tables,
                    lesser + [mirrors[c]],
                    [piece] * groups,
                )
            )
            left_side = all_times(sigma)
            product = jnp.einsum(
                "krs,ksc->krc",
                left_side,
                right_side,
                precision=lax.Precision.HIGH,
                preferred_element_type=jnp.float32,
            )
            top, bottom = product[:, :chunk_rows], product[:, chunk_rows:]
            real = top[:, :, :part_cols] - bottom[:, :, part_cols:]
            imag = top[:, :, part_cols:] + bottom[:, :, :part_cols]
            hub = chunk_of(hub_free, 1, c) + jnp.concatenate([real, imag], axis=2)
            hub_chunks.append(hub)
            tiles = [
                jnp.stack(
                    [
                        lax.slice_in_dim(hub, col, col + tile_cols, axis=2)
                        for col in (d * tile_cols, part_cols + d * tile_cols)
                    ]
                )
                for d in range(half)
            ]
            next_greens.append(outward(tiles))
        greens = next_greens
        if sweep < ITERS - 1:
            whole = unrotate(jnp.concatenate(hub_chunks, axis=1), 1)
            right_side = lax.all_gather(whole, "tcol", axis=1, tiled=True)
    return unrotate(jnp.concatenate(greens, axis=2), 2)


def solution(mesh):
    placed = (P(None, "mom", "tcol", "trow"), P(None, "mom", "tcol", "trow"), P(), P())
    return jax.shard_map(
        body, mesh=mesh, in_specs=placed, out_specs=P(None, "mom", "tcol", "trow"), check_vma=False
    )
```

time: 699 us -> 590 us (0.84)
  starting transfers between devices: 10 us -> 167 us
  waiting for transfers between devices: 380 us -> 251 us
  blocking collectives: 92.4 us -> 0 us
  matrix products: 131 us -> 73.1 us
  Pallas kernels: 0 us -> 15.6 us
  local copies, waits for them, and re-layouts: 43.7 us -> 34.5 us
    all_gather x4 -> x2, waiting for transfers between devices: 341 us -> 0.02 us  [the longest x1 0.02 us: body(): right_side = lax.all_gather(whole, 'tcol', axis=1, tiled=True)]
    ppermute x0 -> x93, waiting for transfers between devices: none -> 251 us  [the longest x8 155 us: outward(): moving = lax.ppermute(moving, 'trow', pairs)]
    ppermute x0 -> x93, starting transfers between devices: none -> 167 us  [the longest x60 90 us: shifted(): lax.ppermute(value, 'mom', [(i, (i + by) % groups) for i in range(groups)])]
    all_to_all x3 -> x0, blocking collectives: 92.4 us -> none  [the longest x2 60 us: body(): lax.all_to_all(sigma_sigma_slab.reshape(2, momenta, 1, piece_width), 'mom...]
    dot_general x28 -> x8, matrix products: 131 us -> 73.1 us  [body(): jnp.einsum('krs,ksc->krc', left_side, right_side, precision=lax.Precision...]
    all_to_all x2 -> x0, waiting for transfers between devices: 37.1 us -> none  [the longest x1 19.4 us: body(): lax.all_to_all(to_slabs(green_now), 'mom', split_axis=2, concat_axis=1, t...]
    reshape x10 -> x0, local copies, waits for them, and re-layouts: 31.1 us -> none  [the longest x6 20.8 us: to_slabs(): return tile.reshape(2, local_mom, groups, slab_width)]
    mul x2 -> x3, other arithmetic: 18.9 us -> 2.75 us  [the longest x2 2.64 us: all_times(): joined = jnp.concatenate(blocks, axis=3) * weights]
  transfers between devices with their start and end apart: 6 -> 95, of which waited for: 6 -> 27; matrix products, arithmetic and copies ran while one was open for 5% -> 6% of each run, Pallas kernels for 0% -> 3%
where the time goes in v1:
time: 590 us; the launch traced here: 581 us
  waiting for transfers between devices  251 us (43%)
  starting transfers between devices  167 us (28%)
  matrix products  73.1 us (12%)
  local copies, waits for them, and re-layouts  34.5 us (6%)
  other arithmetic  24.1 us (4%)
  between operations  15.7 us (3%)
  Pallas kernels  15.6 us (3%)
    ppermute x8, waiting for transfers between devices, outward(): moving = lax.ppermute(moving, 'trow', pairs)  155 us
    ppermute x60, starting transfers between devices, shifted(): lax.ppermute(value, 'mom', [(i, (i + by) % groups) for i in range(groups)])  90 us
    ppermute x9, waiting for transfers between devices, near_tiles(): tiles.append(lax.ppermute(tiles[-1], 'trow', inward))  78.5 us
    dot_general x8, matrix products, body(): jnp.einsum('krs,ksc->krc', left_side, right_side, precision=lax.Precision...  73.1 us
    ppermute x9, starting transfers between devices, near_tiles(): tiles.append(lax.ppermute(tiles[-1], 'trow', inward))  54.7 us
    ppermute x60, waiting for transfers between devices, shifted(): lax.ppermute(value, 'mom', [(i, (i + by) % groups) for i in range(groups)])  17.8 us
    pallas_call x12, Pallas kernels, call_local(): pl.pallas_call(kernel, out_shape=[jax.ShapeDtypeStruct(s, jnp.float32) fo...  15.6 us
    unnamed x102, local copies, waits for them, and re-layouts  13.5 us
  transfers between devices with their start and end apart: 95, of which 27 were waited for; matrix products, arithmetic and copies ran while one was open for 6% of the time, Pallas kernels for 3%

profile of v1, /device:TPU:0, one launch (start us, length us, event | category | flops | bytes accessed | tf_op | source)
XLA Modules:
  0.0 580.8 jit_solution(3019662859628145631)
XLA Ops:
  14.9 47.3 %collective-permute-done = f32[2,1,768,384]{3,2,1,0:T(8,128)S(1)} collective-permute-done((f32[2,1,768,384]{3,2,1,0:T(8,128)}, f32[2,1,768,384]{3,2,1,0:T(8,128)S(1)}, u32[]{:S(2)}, u32[]{:S(2)}) %collective-permute-start) | collective-permute-done | bytes 2359328 | tf_op jit(solution)/shard_map/ppermute | solution.py:191
  143.9 6.4 %collective-permute-start.56 = (f32[2,1,192,384]{3,2,1,0:T(8,128)S(1)}, f32[2,1,192,384]{3,2,1,0:T(8,128)S(1)}, u32[]{:S(2)}, u32[]{:S(2)}) collective-permute-start(f32[2,1,192,384]{3,2,1,0:T(8,128)S(1)} %constant_dynamic-update-slice_fusion.16), channel_id=1, source_target_pairs={{0,2},{6,4},{1,3},{7,5},{8,10},{14,12},{9,11},{15,13},{16,18},{22,... | collective-permute-start | bytes 1769480 | tf_op jit(solution)/shard_map/ppermute | solution.py:191
  165.6 11.8 %collective-permute-start.10 = (f32[2,1,192,384]{3,2,1,0:T(8,128)S(1)}, f32[2,1,192,384]{3,2,1,0:T(8,128)S(1)}, u32[]{:S(2)}, u32[]{:S(2)}) collective-permute-start(f32[2,1,192,384]{3,2,1,0:T(8,128)S(1)} %constant_dynamic-update-slice_fusion), channel_id=1, source_target_pairs={{0,2},{6,4},{1,3},{7,5},{8,10},{14,12},{9,11},{15,13},{16,18},{22,... | collective-permute-start | bytes 1769480 | tf_op jit(solution)/shard_map/ppermute | solution.py:191
  179.0 8.6 %collective-permute-done.32 = f32[2,1,192,384]{3,2,1,0:T(8,128)S(1)} collective-permute-done((f32[2,1,192,384]{3,2,1,0:T(8,128)S(1)}, f32[2,1,192,384]{3,2,1,0:T(8,128)S(1)}, u32[]{:S(2)}, u32[]{:S(2)}) %collective-permute-start.32) | collective-permute-done | bytes 589856 | tf_op jit(solution)/shard_map/ppermute | solution.py:191
  188.4 7.1 %collective-permute-done.10 = f32[2,1,192,384]{3,2,1,0:T(8,128)S(1)} collective-permute-done((f32[2,1,192,384]{3,2,1,0:T(8,128)S(1)}, f32[2,1,192,384]{3,2,1,0:T(8,128)S(1)}, u32[]{:S(2)}, u32[]{:S(2)}) %collective-permute-start.10) | collective-permute-done | bytes 589856 | tf_op jit(solution)/shard_map/ppermute | solution.py:191
  208.1 9.7 %fusion.27 = f32[1,384,1536]{2,1,0:T(8,128)S(1)} fusion(f32[1,1536,1536]{2,1,0:T(8,128)} %all-gather.3.cloned.1.call-done, f32[1,192,1536]{2,1,0:T(8,128)} %get-tuple-element.133, f32[1,192,1536]{2,1,0:T(8,128)} %get-tuple-element.132), kind=kOutput, calls=%fused_computation.45 | convolution fusion | flops 5436407808 | bytes 14155776 | tf_op jit(solution)/shard_map/krs,ksc->krc/dot_general | solution.py:246
  219.4 6.8 %fusion.30 = f32[1,384,1536]{2,1,0:T(8,128)S(1)} fusion(f32[1,1536,1536]{2,1,0:T(8,128)S(1)} %copy-done.33, f32[1,192,1536]{2,1,0:T(8,128)S(1)} %copy-done.13, f32[1,192,1536]{2,1,0:T(8,128)S(1)} %copy-done.14), kind=kOutput, calls=%fused_computation.46 | convolution fusion | flops 5436407808 | bytes 14155776 | tf_op jit(solution)/shard_map/krs,ksc->krc/dot_general | solution.py:246
  227.8 6.8 %fusion.33 = f32[1,384,1536]{2,1,0:T(8,128)S(1)} fusion(f32[1,1536,1536]{2,1,0:T(8,128)S(1)} %copy-done.33, f32[1,192,1536]{2,1,0:T(8,128)S(1)} %copy-done.12, f32[1,192,1536]{2,1,0:T(8,128)S(1)} %copy-done.11), kind=kOutput, calls=%fused_computation.47 | convolution fusion | flops 5436407808 | bytes 14155776 | tf_op jit(solution)/shard_map/krs,ksc->krc/dot_general | solution.py:246
  235.9 17.3 %fusion.24 = f32[1,384,1536]{2,1,0:T(8,128)S(1)} fusion(f32[1,1536,1536]{2,1,0:T(8,128)} %all-gather.3.cloned.1.call-done, f32[1,192,1536]{2,1,0:T(8,128)S(1)} %get-tuple-element.244, f32[1,192,1536]{2,1,0:T(8,128)S(1)} %copy-done.10), kind=kOutput, calls=%fused_computation.44 | convolution fusion | flops 5436407808 | bytes 14155776 | tf_op jit(solution)/shard_map/krs,ksc->krc/dot_general | solution.py:246
  268.8 50.7 %collective-permute-done.82 = f32[2,1,192,384]{3,2,1,0:T(8,128)} collective-permute-done((f32[2,1,192,384]{3,2,1,0:T(8,128)}, f32[2,1,192,384]{3,2,1,0:T(8,128)}, u32[]{:S(2)}, u32[]{:S(2)}) %collective-permute-start.82) | collective-permute-done | bytes 589856 | tf_op jit(solution)/shard_map/ppermute | solution.py:207
  323.2 9.0 %collective-permute-done.71 = f32[2,1,192,384]{3,2,1,0:T(8,128)} collective-permute-done((f32[2,1,192,384]{3,2,1,0:T(8,128)}, f32[2,1,192,384]{3,2,1,0:T(8,128)}, u32[]{:S(2)}, u32[]{:S(2)}) %collective-permute-start.71) | collective-permute-done | bytes 589856 | tf_op jit(solution)/shard_map/ppermute | solution.py:207
  335.1 9.0 %collective-permute-done.60 = f32[2,1,192,384]{3,2,1,0:T(8,128)S(1)} collective-permute-done((f32[2,1,192,384]{3,2,1,0:T(8,128)S(1)}, f32[2,1,192,384]{3,2,1,0:T(8,128)S(1)}, u32[]{:S(2)}, u32[]{:S(2)}) %collective-permute-start.60) | collective-permute-done | bytes 589856 | tf_op jit(solution)/shard_map/ppermute | solution.py:207
  373.1 7.4 %collective-permute-start.75 = (f32[2,1,48,384]{3,2,1,0:T(8,128)S(1)}, f32[2,1,48,384]{3,2,1,0:T(8,128)S(1)}, u32[]{:S(2)}, u32[]{:S(2)}) collective-permute-start(f32[2,1,48,384]{3,2,1,0:T(8,128)S(1)} %get-tuple-element.63), channel_id=1, source_target_pairs={{0,24},{8,0},{16,8},{24,16},{1,25},{9,1},{17,9},{25,17},{2,26},{10... | collective-permute-start | bytes 442376 | tf_op jit(solution)/shard_map/ppermute | solution.py:173
  403.2 6.6 %collective-permute-start.67 = (f32[2,1,192,384]{3,2,1,0:T(8,128)S(1)}, f32[2,1,192,384]{3,2,1,0:T(8,128)S(1)}, u32[]{:S(2)}, u32[]{:S(2)}) collective-permute-start(f32[2,1,192,384]{3,2,1,0:T(8,128)S(1)} %constant_dynamic-update-slice_fusion.20), channel_id=1, source_target_pairs={{0,2},{6,4},{1,3},{7,5},{8,10},{14,12},{9,11},{15,13},{16,18},{22,... | collective-permute-start | bytes 1769480 | tf_op jit(solution)/shard_map/ppermute | solution.py:191
  410.6 11.8 %collective-permute-start.20 = (f32[2,1,192,384]{3,2,1,0:T(8,128)S(1)}, f32[2,1,192,384]{3,2,1,0:T(8,128)S(1)}, u32[]{:S(2)}, u32[]{:S(2)}) collective-permute-start(f32[2,1,192,384]{3,2,1,0:T(8,128)S(1)} %constant_dynamic-update-slice_fusion.4), channel_id=1, source_target_pairs={{0,2},{6,4},{1,3},{7,5},{8,10},{14,12},{9,11},{15,13},{16,18},{22,... | collective-permute-start | bytes 1769480 | tf_op jit(solution)/shard_map/ppermute | solution.py:191
  424.1 9.9 %collective-permute-done.67 = f32[2,1,192,384]{3,2,1,0:T(8,128)S(1)} collective-permute-done((f32[2,1,192,384]{3,2,1,0:T(8,128)S(1)}, f32[2,1,192,384]{3,2,1,0:T(8,128)S(1)}, u32[]{:S(2)}, u32[]{:S(2)}) %collective-permute-start.67) | collective-permute-done | bytes 589856 | tf_op jit(solution)/shard_map/ppermute | solution.py:191
  447.5 9.7 %fusion.45 = f32[1,384,1536]{2,1,0:T(8,128)S(1)} fusion(f32[1,1536,1536]{2,1,0:T(8,128)} %all-gather.5.cloned.1.call-done, f32[1,192,1536]{2,1,0:T(8,128)} %get-tuple-element.93, f32[1,192,1536]{2,1,0:T(8,128)} %get-tuple-element.92), kind=kOutput, calls=%fused_computation.51 | convolution fusion | flops 5436407808 | bytes 14155776 | tf_op jit(solution)/shard_map/krs,ksc->krc/dot_general | solution.py:246
  458.8 6.8 %fusion.42 = f32[1,384,1536]{2,1,0:T(8,128)S(1)} fusion(f32[1,1536,1536]{2,1,0:T(8,128)S(1)} %copy-done.34, f32[1,192,1536]{2,1,0:T(8,128)S(1)} %copy-done.25, f32[1,192,1536]{2,1,0:T(8,128)S(1)} %copy-done.24), kind=kOutput, calls=%fused_computation.50 | convolution fusion | flops 5436407808 | bytes 14155776 | tf_op jit(solution)/shard_map/krs,ksc->krc/dot_general | solution.py:246
  466.9 6.8 %fusion.39 = f32[1,384,1536]{2,1,0:T(8,128)S(1)} fusion(f32[1,1536,1536]{2,1,0:T(8,128)S(1)} %copy-done.34, f32[1,192,1536]{2,1,0:T(8,128)S(1)} %copy-done.23, f32[1,192,1536]{2,1,0:T(8,128)S(1)} %get-tuple-element.84), kind=kOutput, calls=%fused_computation.49 | convolution fusion | flops 5436407808 | bytes 14155776 | tf_op jit(solution)/shard_map/krs,ksc->krc/dot_general | solution.py:246
  473.9 9.3 %fusion.36 = f32[1,384,1536]{2,1,0:T(8,128)S(1)} fusion(f32[1,1536,1536]{2,1,0:T(8,128)} %all-gather.5.cloned.1.call-done, f32[1,192,1536]{2,1,0:T(8,128)S(1)} %get-tuple-element.81, f32[1,192,1536]{2,1,0:T(8,128)S(1)} %get-tuple-element.80), kind=kOutput, calls=%fused_computation.48 | convolution fusion | flops 5436407808 | bytes 14155776 | tf_op jit(solution)/shard_map/krs,ksc->krc/dot_general | solution.py:246
  489.8 54.6 %collective-permute-done.59 = f32[2,1,192,384]{3,2,1,0:T(8,128)S(1)} collective-permute-done((f32[2,1,192,384]{3,2,1,0:T(8,128)S(1)}, f32[2,1,192,384]{3,2,1,0:T(8,128)S(1)}, u32[]{:S(2)}, u32[]{:S(2)}) %collective-permute-start.59) | collective-permute-done | bytes 589856 | tf_op jit(solution)/shard_map/ppermute | solution.py:207
  544.6 12.5 %collective-permute-done.70 = f32[2,1,192,384]{3,2,1,0:T(8,128)S(1)} collective-permute-done((f32[2,1,192,384]{3,2,1,0:T(8,128)S(1)}, f32[2,1,192,384]{3,2,1,0:T(8,128)S(1)}, u32[]{:S(2)}, u32[]{:S(2)}) %collective-permute-start.70) | collective-permute-done | bytes 589856 | tf_op jit(solution)/shard_map/ppermute | solution.py:207
  557.2 8.1 %collective-permute-done.81 = f32[2,1,192,384]{3,2,1,0:T(8,128)S(1)} collective-permute-done((f32[2,1,192,384]{3,2,1,0:T(8,128)S(1)}, f32[2,1,192,384]{3,2,1,0:T(8,128)S(1)}, u32[]{:S(2)}, u32[]{:S(2)}) %collective-permute-start.81) | collective-permute-done | bytes 589856 | tf_op jit(solution)/shard_map/ppermute | solution.py:207
  565.4 6.2 %collective-permute-done.92 = f32[2,1,192,384]{3,2,1,0:T(8,128)S(1)} collective-permute-done((f32[2,1,192,384]{3,2,1,0:T(8,128)S(1)}, f32[2,1,192,384]{3,2,1,0:T(8,128)S(1)}, u32[]{:S(2)}, u32[]{:S(2)}) %collective-permute-start.92) | collective-permute-done | bytes 589856 | tf_op jit(solution)/shard_map/ppermute | solution.py:207
  (383 shorter events, 225.0 us)
Async XLA Ops:
  6.5 201.5 %all-gather.3.cloned.1.call-start = ((), (), s32[]{:S(2)}) async-start(), calls=%async_computation | async-start | bytes 14155776 | tf_op jit(solution)/shard_map/all_gather | solution.py:222
  6.5 55.7 %collective-permute-start = (f32[2,1,768,384]{3,2,1,0:T(8,128)}, f32[2,1,768,384]{3,2,1,0:T(8,128)S(1)}, u32[]{:S(2)}, u32[]{:S(2)}) collective-permute-start(f32[2,1,768,384]{3,2,1,0:T(8,128)} %param.6), channel_id=1, source_target_pairs={{0,2},{6,4},{1,3},{7,5},{8,10},{14,12},{9,11},{15,13},{16,18},{22,... | collective-permute-start | bytes 7077896 | tf_op jit(solution)/shard_map/ppermute | solution.py:191
  66.8 380.7 %all-gather.5.cloned.1.call-start = ((), (), s32[]{:S(2)}) async-start(), calls=%async_computation.1 | async-start | bytes 14155776 | tf_op jit(solution)/shard_map/all_gather | solution.py:271
  143.9 20.9 %collective-permute-start.56 = (f32[2,1,192,384]{3,2,1,0:T(8,128)S(1)}, f32[2,1,192,384]{3,2,1,0:T(8,128)S(1)}, u32[]{:S(2)}, u32[]{:S(2)}) collective-permute-start(f32[2,1,192,384]{3,2,1,0:T(8,128)S(1)} %constant_dynamic-update-slice_fusion.16), channel_id=1, source_target_pairs={{0,2},{6,4},{1,3},{7,5},{8,10},{14,12},{9,11},{15,13},{16,18},{22,... | collective-permute-start | bytes 1769480 | tf_op jit(solution)/shard_map/ppermute | solution.py:191
  155.5 22.0 %collective-permute-start.44 = (f32[2,1,192,384]{3,2,1,0:T(8,128)S(1)}, f32[2,1,192,384]{3,2,1,0:T(8,128)S(1)}, u32[]{:S(2)}, u32[]{:S(2)}) collective-permute-start(f32[2,1,192,384]{3,2,1,0:T(8,128)S(1)} %constant_dynamic-update-slice_fusion.12), channel_id=1, source_target_pairs={{0,2},{6,4},{1,3},{7,5},{8,10},{14,12},{9,11},{15,13},{16,18},{22,... | collective-permute-start | bytes 1769480 | tf_op jit(solution)/shard_map/ppermute | solution.py:191
  158.6 29.0 %collective-permute-start.32 = (f32[2,1,192,384]{3,2,1,0:T(8,128)S(1)}, f32[2,1,192,384]{3,2,1,0:T(8,128)S(1)}, u32[]{:S(2)}, u32[]{:S(2)}) collective-permute-start(f32[2,1,192,384]{3,2,1,0:T(8,128)S(1)} %constant_dynamic-update-slice_fusion.8), channel_id=1, source_target_pairs={{0,2},{6,4},{1,3},{7,5},{8,10},{14,12},{9,11},{15,13},{16,18},{22,... | collective-permute-start | bytes 1769480 | tf_op jit(solution)/shard_map/ppermute | solution.py:191
  164.8 23.5 %collective-permute-start.12 = (f32[2,1,192,384]{3,2,1,0:T(8,128)S(1)}, f32[2,1,192,384]{3,2,1,0:T(8,128)S(1)}, u32[]{:S(2)}, u32[]{:S(2)}) collective-permute-start(f32[2,1,192,384]{3,2,1,0:T(8,128)S(1)} %constant_dynamic-update-slice_fusion), channel_id=1, source_target_pairs={{2,4},{4,2},{3,5},{5,3},{10,12},{12,10},{11,13},{13,11},{18,20},{2... | collective-permute-start | bytes 1769480 | tf_op jit(solution)/shard_map/ppermute | solution.py:196
  165.6 29.9 %collective-permute-start.10 = (f32[2,1,192,384]{3,2,1,0:T(8,128)S(1)}, f32[2,1,192,384]{3,2,1,0:T(8,128)S(1)}, u32[]{:S(2)}, u32[]{:S(2)}) collective-permute-start(f32[2,1,192,384]{3,2,1,0:T(8,128)S(1)} %constant_dynamic-update-slice_fusion), channel_id=1, source_target_pairs={{0,2},{6,4},{1,3},{7,5},{8,10},{14,12},{9,11},{15,13},{16,18},{22,... | collective-permute-start | bytes 1769480 | tf_op jit(solution)/shard_map/ppermute | solution.py:191
  255.9 63.6 %collective-permute-start.82 = (f32[2,1,192,384]{3,2,1,0:T(8,128)}, f32[2,1,192,384]{3,2,1,0:T(8,128)}, u32[]{:S(2)}, u32[]{:S(2)}) collective-permute-start(f32[2,1,192,384]{3,2,1,0:T(8,128)} %pad_maximum_fusion.9), channel_id=1, source_target_pairs={{2,0},{4,6},{3,1},{5,7},{10,8},{12,14},{11,9},{13,15},{18,16},{20,... | collective-permute-start | bytes 1769480 | tf_op jit(solution)/shard_map/ppermute | solution.py:207
  258.9 73.2 %collective-permute-start.71 = (f32[2,1,192,384]{3,2,1,0:T(8,128)}, f32[2,1,192,384]{3,2,1,0:T(8,128)}, u32[]{:S(2)}, u32[]{:S(2)}) collective-permute-start(f32[2,1,192,384]{3,2,1,0:T(8,128)} %pad_maximum_fusion.7), channel_id=1, source_target_pairs={{2,0},{4,6},{3,1},{5,7},{10,8},{12,14},{11,9},{13,15},{18,16},{20,... | collective-permute-start | bytes 1769480 | tf_op jit(solution)/shard_map/ppermute | solution.py:207
  266.0 78.0 %collective-permute-start.60 = (f32[2,1,192,384]{3,2,1,0:T(8,128)S(1)}, f32[2,1,192,384]{3,2,1,0:T(8,128)S(1)}, u32[]{:S(2)}, u32[]{:S(2)}) collective-permute-start(f32[2,1,192,384]{3,2,1,0:T(8,128)S(1)} %pad_maximum_fusion.5), channel_id=1, source_target_pairs={{2,0},{4,6},{3,1},{5,7},{10,8},{12,14},{11,9},{13,15},{18,16},{20,... | collective-permute-start | bytes 1769480 | tf_op jit(solution)/shard_map/ppermute | solution.py:207
  267.5 82.8 %collective-permute-start.13 = (f32[2,1,192,384]{3,2,1,0:T(8,128)S(1)}, f32[2,1,192,384]{3,2,1,0:T(8,128)S(1)}, u32[]{:S(2)}, u32[]{:S(2)}) collective-permute-start(f32[2,1,192,384]{3,2,1,0:T(8,128)S(1)} %pad_maximum_fusion.3), channel_id=1, source_target_pairs={{2,0},{4,6},{3,1},{5,7},{10,8},{12,14},{11,9},{13,15},{18,16},{20,... | collective-permute-start | bytes 1769480 | tf_op jit(solution)/shard_map/ppermute | solution.py:207
  320.8 30.3 %collective-permute-start.83 = (f32[2,1,48,384]{3,2,1,0:T(8,128)S(1)}, f32[2,1,48,384]{3,2,1,0:T(8,128)S(1)}, u32[]{:S(2)}, u32[]{:S(2)}) collective-permute-start(f32[2,1,48,384]{3,2,1,0:T(8,128)S(1)} %get-tuple-element.228), channel_id=1, source_target_pairs={{0,8},{8,16},{16,24},{24,0},{1,9},{9,17},{17,25},{25,1},{2,10},{10... | collective-permute-start | bytes 442376 | tf_op jit(solution)/shard_map/ppermute | solution.py:173
  321.8 32.4 %collective-permute-start.84 = (f32[2,1,48,384]{3,2,1,0:T(8,128)S(1)}, f32[2,1,48,384]{3,2,1,0:T(8,128)S(1)}, u32[]{:S(2)}, u32[]{:S(2)}) collective-permute-start(f32[2,1,48,384]{3,2,1,0:T(8,128)S(1)} %get-tuple-element.227), channel_id=1, source_target_pairs={{0,16},{8,24},{16,0},{24,8},{1,17},{9,25},{17,1},{25,9},{2,18},{10... | collective-permute-start | bytes 442376 | tf_op jit(solution)/shard_map/ppermute | solution.py:173
  332.1 22.4 %collective-permute-start.85 = (f32[2,1,48,384]{3,2,1,0:T(8,128)S(1)}, f32[2,1,48,384]{3,2,1,0:T(8,128)S(1)}, u32[]{:S(2)}, u32[]{:S(2)}) collective-permute-start(f32[2,1,48,384]{3,2,1,0:T(8,128)S(1)} %get-tuple-element.226), channel_id=1, source_target_pairs={{0,24},{8,0},{16,8},{24,16},{1,25},{9,1},{17,9},{25,17},{2,26},{10... | collective-permute-start | bytes 442376 | tf_op jit(solution)/shard_map/ppermute | solution.py:173
  400.4 22.0 %collective-permute-start.78 = (f32[2,1,192,384]{3,2,1,0:T(8,128)S(1)}, f32[2,1,192,384]{3,2,1,0:T(8,128)S(1)}, u32[]{:S(2)}, u32[]{:S(2)}) collective-permute-start(f32[2,1,192,384]{3,2,1,0:T(8,128)S(1)} %constant_dynamic-update-slice_fusion.24), channel_id=1, source_target_pairs={{0,2},{6,4},{1,3},{7,5},{8,10},{14,12},{9,11},{15,13},{16,18},{22,... | collective-permute-start | bytes 1769480 | tf_op jit(solution)/shard_map/ppermute | solution.py:191
  402.5 20.8 %collective-permute-start.69 = (f32[2,1,192,384]{3,2,1,0:T(8,128)S(1)}, f32[2,1,192,384]{3,2,1,0:T(8,128)S(1)}, u32[]{:S(2)}, u32[]{:S(2)}) collective-permute-start(f32[2,1,192,384]{3,2,1,0:T(8,128)S(1)} %constant_dynamic-update-slice_fusion.20), channel_id=1, source_target_pairs={{2,4},{4,2},{3,5},{5,3},{10,12},{12,10},{11,13},{13,11},{18,20},{2... | collective-permute-start | bytes 1769480 | tf_op jit(solution)/shard_map/ppermute | solution.py:196
  403.2 30.8 %collective-permute-start.67 = (f32[2,1,192,384]{3,2,1,0:T(8,128)S(1)}, f32[2,1,192,384]{3,2,1,0:T(8,128)S(1)}, u32[]{:S(2)}, u32[]{:S(2)}) collective-permute-start(f32[2,1,192,384]{3,2,1,0:T(8,128)S(1)} %constant_dynamic-update-slice_fusion.20), channel_id=1, source_target_pairs={{0,2},{6,4},{1,3},{7,5},{8,10},{14,12},{9,11},{15,13},{16,18},{22,... | collective-permute-start | bytes 1769480 | tf_op jit(solution)/shard_map/ppermute | solution.py:191
  409.8 24.9 %collective-permute-start.22 = (f32[2,1,192,384]{3,2,1,0:T(8,128)S(1)}, f32[2,1,192,384]{3,2,1,0:T(8,128)S(1)}, u32[]{:S(2)}, u32[]{:S(2)}) collective-permute-start(f32[2,1,192,384]{3,2,1,0:T(8,128)S(1)} %constant_dynamic-update-slice_fusion.4), channel_id=1, source_target_pairs={{2,4},{4,2},{3,5},{5,3},{10,12},{12,10},{11,13},{13,11},{18,20},{2... | collective-permute-start | bytes 1769480 | tf_op jit(solution)/shard_map/ppermute | solution.py:196
  410.6 29.7 %collective-permute-start.20 = (f32[2,1,192,384]{3,2,1,0:T(8,128)S(1)}, f32[2,1,192,384]{3,2,1,0:T(8,128)S(1)}, u32[]{:S(2)}, u32[]{:S(2)}) collective-permute-start(f32[2,1,192,384]{3,2,1,0:T(8,128)S(1)} %constant_dynamic-update-slice_fusion.4), channel_id=1, source_target_pairs={{0,2},{6,4},{1,3},{7,5},{8,10},{14,12},{9,11},{15,13},{16,18},{22,... | collective-permute-start | bytes 1769480 | tf_op jit(solution)/shard_map/ppermute | solution.py:191
  484.2 60.2 %collective-permute-start.59 = (f32[2,1,192,384]{3,2,1,0:T(8,128)S(1)}, f32[2,1,192,384]{3,2,1,0:T(8,128)S(1)}, u32[]{:S(2)}, u32[]{:S(2)}) collective-permute-start(f32[2,1,192,384]{3,2,1,0:T(8,128)S(1)} %pad_maximum_fusion.4), channel_id=1, source_target_pairs={{2,0},{4,6},{3,1},{5,7},{10,8},{12,14},{11,9},{13,15},{18,16},{20,... | collective-permute-start | bytes 1769480 | tf_op jit(solution)/shard_map/ppermute | solution.py:207
  485.6 71.4 %collective-permute-start.70 = (f32[2,1,192,384]{3,2,1,0:T(8,128)S(1)}, f32[2,1,192,384]{3,2,1,0:T(8,128)S(1)}, u32[]{:S(2)}, u32[]{:S(2)}) collective-permute-start(f32[2,1,192,384]{3,2,1,0:T(8,128)S(1)} %pad_maximum_fusion.6), channel_id=1, source_target_pairs={{2,0},{4,6},{3,1},{5,7},{10,8},{12,14},{11,9},{13,15},{18,16},{20,... | collective-permute-start | bytes 1769480 | tf_op jit(solution)/shard_map/ppermute | solution.py:207
  487.1 78.2 %collective-permute-start.81 = (f32[2,1,192,384]{3,2,1,0:T(8,128)S(1)}, f32[2,1,192,384]{3,2,1,0:T(8,128)S(1)}, u32[]{:S(2)}, u32[]{:S(2)}) collective-permute-start(f32[2,1,192,384]{3,2,1,0:T(8,128)S(1)} %pad_maximum_fusion.8), channel_id=1, source_target_pairs={{2,0},{4,6},{3,1},{5,7},{10,8},{12,14},{11,9},{13,15},{18,16},{20,... | collective-permute-start | bytes 1769480 | tf_op jit(solution)/shard_map/ppermute | solution.py:207
  488.5 83.1 %collective-permute-start.92 = (f32[2,1,192,384]{3,2,1,0:T(8,128)S(1)}, f32[2,1,192,384]{3,2,1,0:T(8,128)S(1)}, u32[]{:S(2)}, u32[]{:S(2)}) collective-permute-start(f32[2,1,192,384]{3,2,1,0:T(8,128)S(1)} %pad_maximum_fusion.10), channel_id=1, source_target_pairs={{2,0},{4,6},{3,1},{5,7},{10,8},{12,14},{11,9},{13,15},{18,16},{20,... | collective-permute-start | bytes 1769480 | tf_op jit(solution)/shard_map/ppermute | solution.py:207
  (110 other events, 1262.1 us)
Sparse Core Ops, SparseCore 0:
  66.9 22.8 all-gather.2
  265.0 69.1 all-gather.4
